TPU v7x, 128 devices: a whole 4x4x4 slice. The times are simulated.
128 devices in a mesh: dp: 16 (over x, y), red: 8 (over z, core).
Axes of the slice: x: 4, y: 4, z: 4, core: 2. Of those that a mesh axis runs over, the one named last changes fastest.
Arguments:
- frames: bfloat16 [2048, 48, 1536], P(('dp', 'red')), may hold values from -36 to 36
- cotangent: bfloat16 [2048, 48, 1536], P(('dp', 'red')), may hold values from -6 to 6
- w_in: bfloat16 [1536, 3072], P('red'), may hold values from -0.15625 to 0.15625
- kernel: float32 [31, 1536], replicated, may hold values from -1 to 1
- gain: float32 [1536], replicated, may hold values from 0.25 to 1.75
- lengths: int32 [2048], replicated, may hold values from 1 to 47, as said below
Outputs:
- module_output: bfloat16 [2048, 48, 1536], P(('dp', 'red'))
- frame_gradient: bfloat16 [2048, 48, 1536], P(('dp', 'red'))
- grad_w_in: float32 [1536, 3072], P('red')
- grad_kernel: float32 [31, 1536], replicated
- grad_gain: float32 [1536], replicated
Inputs may be any that keep to these rules, and one draw needn't show every extreme that they name: The slots of each device, in order, form 16 groups of 1 slots. The q-th slot of group j on the device with dp index i and red index r and the q-th slot of group j on the device with dp index (2 j + 1 - i) mod 16 and the same red index have lengths that sum to exactly 48. The slots of dp index 0 all hold at least three quarters of 48 frames, rounded up.
All inputs are finite; a program needn't handle non-finite values.
Results may differ from a plain program's by a relative error of at most 0.0054.
Values may be sent and summed in bfloat16 or wider, within the bound.
A program may use at most 128 MiB of HBM per device.

v0:
```python
import jax
import jax.numpy as jnp
from jax import lax
from jax.sharding import PartitionSpec as P

EPSILON = 1e-05


def normalize(widened_frames):
    center = widened_frames - jnp.mean(widened_frames, axis=-1, keepdims=True)
    inv_std = lax.rsqrt(jnp.mean(center * center, axis=-1, keepdims=True) + EPSILON)
    return (center * inv_std, inv_std)


def block_pass(frames, cotangent, valid_frame_mask, segment, weights, kernel, gain):
    row_count, length, model_width = frames.shape
    tap_count = kernel.shape[0]
    reach = tap_count // 2
    widened_frames = frames.astype(jnp.float32)
    normed, inv_std = normalize(widened_frames)
    scaled = (normed * gain).astype(jnp.bfloat16)
    flat_in = scaled.reshape(row_count * length, model_width)
    hidden = jnp.dot(flat_in, weights, preferred_element_type=jnp.float32)
    hidden = hidden.reshape(row_count, length, 2 * model_width)
    value_portion = hidden[..., :model_width]
    gate_sigmoid = jax.nn.sigmoid(hidden[..., model_width:])
    frame_validity = valid_frame_mask.astype(jnp.float32)[..., None]
    gated_linear_output = value_portion * gate_sigmoid * frame_validity
    padded = jnp.pad(gated_linear_output, ((0, 0), (reach, reach), (0, 0)))
    seg_pad = jnp.pad(segment, ((0, 0), (reach, reach)), constant_values=-1)
    convolved_frames = jnp.zeros_like(gated_linear_output)
    for offset in range(tap_count):
        window = padded[:, offset : offset + length]
        same_seg = (seg_pad[:, offset : offset + length] == segment).astype(jnp.float32)[..., None]
        convolved_frames = convolved_frames + kernel[offset] * (window * same_seg)
    swish_activation = jax.nn.sigmoid(convolved_frames)
    module_output = (
        (widened_frames + convolved_frames * swish_activation) * frame_validity
    ).astype(jnp.bfloat16)
    incoming_gradient = cotangent.astype(jnp.float32) * frame_validity
    grad_conv = incoming_gradient * (
        swish_activation * (1.0 + convolved_frames * (1.0 - swish_activation))
    )
    grad_pad = jnp.pad(grad_conv, ((0, 0), (reach, reach), (0, 0)))
    gated_linear_gradient = jnp.zeros_like(gated_linear_output)
    kernel_terms = []
    for offset in range(tap_count):
        window = padded[:, offset : offset + length]
        same_seg = (seg_pad[:, offset : offset + length] == segment).astype(jnp.float32)[..., None]
        kernel_terms.append(jnp.sum(grad_conv * window * same_seg, axis=(0, 1)))
        back_start = 2 * reach - offset
        back_same = (seg_pad[:, back_start : back_start + length] == segment).astype(jnp.float32)[
            ..., None
        ]
        gated_linear_gradient = gated_linear_gradient + kernel[offset] * (
            grad_pad[:, back_start : back_start + length] * back_same
        )
    gated_linear_gradient = gated_linear_gradient * frame_validity
    grad_hidden = jnp.concatenate(
        [
            gated_linear_gradient * gate_sigmoid,
            gated_linear_gradient * value_portion * gate_sigmoid * (1.0 - gate_sigmoid),
        ],
        axis=-1,
    ).astype(jnp.bfloat16)
    flat_grad = grad_hidden.reshape(row_count * length, 2 * model_width)
    grad_scaled = lax.dot_general(
        flat_grad, weights, (((1,), (1,)), ((), ())), preferred_element_type=jnp.float32
    )
    grad_scaled = grad_scaled.reshape(row_count, length, model_width)
    gain_term = jnp.sum(grad_scaled * normed, axis=(0, 1))
    grad_normed = grad_scaled * gain
    frame_gradient = incoming_gradient + inv_std * (
        grad_normed
        - jnp.mean(grad_normed, axis=-1, keepdims=True)
        - normed * jnp.mean(grad_normed * normed, axis=-1, keepdims=True)
    )
    frame_gradient = (frame_gradient * frame_validity).astype(jnp.bfloat16)
    return (module_output, frame_gradient, flat_in, flat_grad, jnp.stack(kernel_terms), gain_term)


def local(frames, cotangent, w_in, kernel, gain, lengths):
    dp_size = lax.axis_size("dp")
    red_size = lax.axis_size("red")
    dp_index = lax.axis_index("dp")
    red_index = lax.axis_index("red")
    local_utts, length, model_width = frames.shape
    weights = lax.all_gather(w_in, "red", axis=0, tiled=True)
    positions = jnp.arange(length, dtype=jnp.int32)
    by_owner = lengths.reshape(dp_size, red_size, local_utts)
    own_lengths = lax.dynamic_slice(by_owner, (dp_index, red_index, 0), (1, 1, local_utts)).reshape(
        local_utts
    )
    valid_frame_mask = positions[None, :] < own_lengths[:, None]
    segment = jnp.where(valid_frame_mask, 0, 1).astype(jnp.int32)
    module_output, frame_gradient, flat_in, flat_grad, kernel_part, gain_part = block_pass(
        frames, cotangent, valid_frame_mask, segment, weights, kernel, gain
    )
    grad_scale = lax.rsqrt(jnp.sum(lengths).astype(jnp.float32))
    block_rows = model_width // (dp_size * red_size)
    ordered = flat_in.reshape(-1, red_size, dp_size, block_rows)
    ordered = jnp.transpose(ordered, (0, 2, 1, 3)).reshape(-1, model_width)
    owned_rows = lax.psum_scatter(
        lax.dot_general(
            ordered, flat_grad, (((0,), (0,)), ((), ())), preferred_element_type=jnp.float32
        ),
        ("dp", "red"),
        scatter_dimension=0,
        tiled=True,
    )
    grad_weights = lax.all_gather(owned_rows, "dp", axis=0, tiled=True)
    kernel_total, gain_total = lax.psum((kernel_part, gain_part), ("dp", "red"))
    return (
        module_output,
        frame_gradient,
        grad_weights * grad_scale,
        kernel_total * grad_scale,
        gain_total * grad_scale,
    )


def solution(mesh):
    placed = (
        P(("dp", "red"), None, None),
        P(("dp", "red"), None, None),
        P("red", None),
        P(),
        P(),
        P(),
    )
    return jax.shard_map(
        local,
        mesh=mesh,
        in_specs=placed,
        out_specs=(
            P(("dp", "red"), None, None),
            P(("dp", "red"), None, None),
            P("red", None),
            P(),
            P(),
        ),
        check_vma=False,
    )
```

profile of v0, /device:TPU:1, one launch (start us, length us, event | category | flops | bytes accessed | tf_op | source)
XLA Modules:
  0.0 923.5 jit_solution(477016552205187638)
XLA Ops:
  8.8 2.1 convert_reduce_fusion
  12.2 2.2 fusion.11
  14.4 8.3 copy.13
  22.7 10.7 %reshape_reshape.3 = bf16[768,8,16,12]{0,3,2,1:T(8,128)(2,1)} reshape(bf16[16,48,1536]{1,0,2:T(8,128)(2,1)} %copy.13) | data formatting | bytes 4718592 | tf_op jit(solution)/shard_map/reshape;reshape | solution.py:101
  33.4 4.0 copy.14
  37.4 5.2 reshape.139
  43.8 23.9 %all-gather.4.cloned.1.call-done = bf16[1536,3072]{1,0:T(8,128)(2,1)} async-done(((bf16[192,3072]{1,0:T(8,128)(2,1)}), bf16[1536,3072]{1,0:T(8,128)(2,1)}) %all-gather.4.cloned.1.call-update) | async-done | bytes 9437200 | tf_op jit(solution)/shard_map/all_gather | solution.py:88
  67.7 10.8 %fusion.3 = f32[16,48,3072]{2,1,0:T(8,128)S(1)} fusion(bf16[16,48,1536]{2,1,0:T(8,128)(2,1)} %fusion.11, bf16[1536,3072]{1,0:T(8,128)(2,1)} %all-gather.4.cloned.1.call-done), kind=kOutput, calls=%fused_computation.62 | convolution fusion | flops 7247757312 | bytes 21233664 | tf_op jit(solution)/shard_map/dot_general | solution.py:23
  79.9 2.7 copy-done.3
  82.6 49.2 %multiply_reduce_fusion = (f32[1536]{0:T(1024)}, f32[1536]{0:T(1024)}, f32[1536]{0:T(1024)}, f32[1536]{0:T(1024)}, f32[1536]{0:T(1024)}, /*index=5*/f32[1536]{0:...) fusion(f32[16,48,1536]{2,1,0:T(8,128)S(1)} %multiply_multiply_f, ...), kind=kLoop, calls=%fused_computation.186 | loop fusion | flops 150981120 | bytes 16856064 | tf_op jit(solution)/shard_map/reduce_sum | solution.py:50
  132.0 28.6 %multiply_convert_fusion.1 = (bf16[16,48,1536]{2,1,0:T(8,128)(2,1)S(1)}, f32[16,48,1536]{2,1,0:T(8,128)}) fusion(f32[16,48,3072]{2,1,0:T(8,128)} %copy-done.3, f32[16,48]{1,0:T(8,128)S(1)} %get-tuple-element.106, f32[16,48]{1,0:T(8,128)S(1)} %get-tuple-element.76, f32[1536]{0:T(1024)} %copy-done.57, f32[16,48]{1,0:T(8,128)S(1)} %get-tuple-element.77, ...), kind=kLoop, calls=%fused_computation.218 | loop fusion | flops 114425856 | bytes 16800768 | tf_op jit(solution)/shard_map/convert.4
  160.6 6.9 multiply_convert_fusion
  168.9 10.8 %fusion.119 = f32[1536,3072]{1,0:T(8,128)} fusion(bf16[768,1536]{0,1:T(8,128)(2,1)S(1)} %copy-done.8, bf16[768,1536]{1,0:T(8,128)(2,1)S(1)} %bitcast.24, bf16[768,1536]{1,0:T(8,128)(2,1)S(1)} %bitcast.23), kind=kOutput, calls=%fused_computation.182 | convolution fusion | flops 7257194496 | bytes 25952256 | tf_op jit(solution)/shard_map/dot_general | solution.py:104
  179.8 359.8 %fusion = f32[16,3072]{1,0:T(8,128)S(1)} fusion(f32[1536,3072]{1,0:T(8,128)} %fusion.119), kind=kCustom, calls=%all-reduce-scatter | all-reduce-scatter fusion | flops 6291457 | bytes 19070976
  552.0 15.3 %collective-permute-start.22 = (f32[16,3072]{1,0:T(8,128)S(1)}, f32[16,3072]{1,0:T(8,128)S(1)}, u32[]{:S(2)}, u32[]{:S(2)}) collective-permute-start(f32[16,3072]{1,0:T(8,128)S(1)} %fusion), channel_id=1, source_target_pairs={{0,23},{1,24},{2,25},{3,26},{4,27},{5,28},{6,29},{7,30},{8,31},{9,... | collective-permute-start | bytes 589832
  567.3 6.4 collective-permute-start.21
  573.7 5.7 collective-permute-start.20
  579.4 8.4 collective-permute-start.19
  587.8 2.0 collective-permute-start.18
  589.8 5.9 collective-permute-start.17
  595.7 2.0 collective-permute-start.16
  597.7 3.8 collective-permute-start.15
  603.1 5.5 collective-permute-start.14
  608.6 12.3 %collective-permute-start.13 = (f32[16,3072]{1,0:T(8,128)S(1)}, f32[16,3072]{1,0:T(8,128)S(1)}, u32[]{:S(2)}, u32[]{:S(2)}) collective-permute-start(f32[16,3072]{1,0:T(8,128)S(1)} %fusion), channel_id=1, source_target_pairs={{0,14},{1,15},{2,16},{3,17},{4,18},{5,19},{6,20},{7,21},{8,22},{9,... | collective-permute-start | bytes 589832
  620.9 10.3 %collective-permute-start.12 = (f32[16,3072]{1,0:T(8,128)S(1)}, f32[16,3072]{1,0:T(8,128)S(1)}, u32[]{:S(2)}, u32[]{:S(2)}) collective-permute-start(f32[16,3072]{1,0:T(8,128)S(1)} %fusion), channel_id=1, source_target_pairs={{0,13},{1,14},{2,15},{3,16},{4,17},{5,18},{6,19},{7,20},{8,21},{9,... | collective-permute-start | bytes 589832
  631.2 14.7 %collective-permute-start.11 = (f32[16,3072]{1,0:T(8,128)S(1)}, f32[16,3072]{1,0:T(8,128)S(1)}, u32[]{:S(2)}, u32[]{:S(2)}) collective-permute-start(f32[16,3072]{1,0:T(8,128)S(1)} %fusion), channel_id=1, source_target_pairs={{0,12},{1,13},{2,14},{3,15},{4,16},{5,17},{6,18},{7,19},{8,20},{9,... | collective-permute-start | bytes 589832
  647.3 26.0 %multiply_reduce_fusion.9 = (f32[1536]{0:T(1024)S(1)}, f32[1536]{0:T(1024)S(1)}, f32[1536]{0:T(1024)S(1)}, f32[1536]{0:T(1024)S(1)}, f32[1536]{0:T(1024)S(1)}, /...) fusion(f32[16,48,1536]{2,1,0:T(8,128)} %copy-done.1, f32[16,48,1536]{2,1,0:T(8,128)} %copy-done, ...), kind=kLoop, calls=%fused_computation.195 | loop fusion | flops 30657024 | bytes 9517056 | tf_op jit(solution)/shard_map/reduce_sum | solution.py:50
  674.6 5.2 collective-permute-start.8
  679.9 1.9 collective-permute-start.7
  681.8 2.5 collective-permute-start.6
  685.1 2.7 collective-permute-start.5
  687.9 9.0 multiply_reduce_fusion.18
  697.0 6.7 collective-permute-start.4
  703.7 2.0 collective-permute-start.3
  705.7 4.6 collective-permute-start.2
  710.3 2.0 collective-permute-start.1
  712.9 2.1 collective-permute-start
  715.0 3.9 multiply_reduce_fusion.27
  719.5 2.7 stack.127
  722.4 84.8 %concatenate.17 = f32[524,3072]{1,0:T(8,128)} concatenate(f32[12,3072]{1,0:T(8,128)S(1)} %collective-permute-done.31, f32[16,3072]{1,0:T(8,128)S(1)} %collective-permute-done.30, f32[16,3072]{1,0:T(8,128)} %copy-done.9, f32[16,3072]{1,0:T(8,128)} %copy-done.10, f32[16,3072]{1,0:T(8,128)} %copy-done.11, f32[16,3072]{1,0:T(8,128)} %copy-done.12, f32[16,3072]{1,0:T(8,128)} %copy-done.13, ...), dimensions={0} | concatenate | bytes 12877824
  807.2 1.7 dynamic-slice_bitcast_fusion
  808.9 14.3 %fusion.18 = (f32[1536]{0:T(1024)S(1)}, f32[16,48]{1,0:T(8,128)S(1)}, f32[16,48]{1,0:T(8,128)S(1)}, f32[16,48,1536]{2,1,0:T(8,128)}) fusion(bf16[16,48,1536]{2,1,0:T(8,128)(2,1)S(1)} %copy-done.4, f32[16,48]{1,0:T(8,128)S(1)} %copy-done.60, f32[16,48]{1,0:T(8,128)S(1)} %copy-done.52, f32[1536]{0:T(1024)S(1)} %copy-done.62, ...), kind=kOutput, calls=%fused_computation.80 | convolution fusion | flops 7267808256 | bytes 21258240 | tf_op jit(solution)/shard_map/dot_general | solution.py:67
  823.2 63.9 %psum.15 = f32[1536]{0:T(1024)S(1)} all-reduce(f32[1536]{0:T(1024)S(1)} %get-tuple-element.36), channel_id=1, replica_groups=mesh['dp'=16,'red'=8] {'dp','red'}, use_global_device_ids=true, to_apply=%region_39.40 | all-reduce | flops 1536 | bytes 12288 | tf_op jit(solution)/shard_map/psum | solution.py:112
  887.7 7.8 fusion.17
  895.6 1.6 broadcast_multiply_fusion.1
  897.2 12.9 %all-gather.6.cloned.1.call-done = f32[16,12,3072]{2,1,0:T(8,128)} async-done(((f32[1,12,3072]{2,1,0:T(8,128)}), f32[16,12,3072]{2,1,0:T(8,128)}) %all-gather.6.cloned.1.call-update) | async-done | bytes 2359312 | tf_op jit(solution)/shard_map/all_gather | solution.py:111
  910.1 3.9 broadcast_multiply_fusion
  914.0 3.0 reshape.143
  (248 shorter events, 24.7 us)
Async XLA Ops:
  7.2 60.5 %all-gather.4.cloned.1.call-start = ((), (), s32[]{:S(2)}) async-start(), calls=%async_computation | async-start | bytes 10616832 | tf_op jit(solution)/shard_map/all_gather | solution.py:88
  7.9 887.6 %all-reduce.7.cloned.1.call-start = ((), (), s32[]{:S(2)}) async-start(), calls=%async_computation.1 | async-start | bytes 393216 | tf_op jit(solution)/shard_map/psum | solution.py:112
  43.5 88.4 %copy-start.42 = (f32[16,48]{1,0:T(8,128)}, f32[16,48]{1,0:T(8,128)S(1)}, u32[]{:S(2)}) copy-start(f32[16,48]{1,0:T(8,128)S(1)} %get-tuple-element.89) | copy-start | bytes 9220
  43.5 88.4 %copy-start.44 = (f32[16,48]{1,0:T(8,128)}, f32[16,48]{1,0:T(8,128)S(1)}, u32[]{:S(2)}) copy-start(f32[16,48]{1,0:T(8,128)S(1)} %get-tuple-element.90) | copy-start | bytes 9220
  43.5 88.4 %copy-start.45 = (f32[16,48]{1,0:T(8,128)}, f32[16,48]{1,0:T(8,128)S(1)}, u32[]{:S(2)}) copy-start(f32[16,48]{1,0:T(8,128)S(1)} %get-tuple-element.91) | copy-start | bytes 9220
  43.5 88.4 %copy-start.46 = (f32[16,48]{1,0:T(8,128)}, f32[16,48]{1,0:T(8,128)S(1)}, u32[]{:S(2)}) copy-start(f32[16,48]{1,0:T(8,128)S(1)} %get-tuple-element.92) | copy-start | bytes 9220
  43.5 88.4 %copy-start.47 = (f32[16,48]{1,0:T(8,128)}, f32[16,48]{1,0:T(8,128)S(1)}, u32[]{:S(2)}) copy-start(f32[16,48]{1,0:T(8,128)S(1)} %get-tuple-element.93) | copy-start | bytes 9220
  43.6 88.3 %copy-start.48 = (f32[16,48]{1,0:T(8,128)}, f32[16,48]{1,0:T(8,128)S(1)}, u32[]{:S(2)}) copy-start(f32[16,48]{1,0:T(8,128)S(1)} %get-tuple-element.94) | copy-start | bytes 9220
  43.6 88.3 %copy-start.49 = (f32[16,48]{1,0:T(8,128)}, f32[16,48]{1,0:T(8,128)S(1)}, u32[]{:S(2)}) copy-start(f32[16,48]{1,0:T(8,128)S(1)} %get-tuple-element.95) | copy-start | bytes 9220
  43.6 88.3 %copy-start.50 = (f32[16,48]{1,0:T(8,128)}, f32[16,48]{1,0:T(8,128)S(1)}, u32[]{:S(2)}) copy-start(f32[16,48]{1,0:T(8,128)S(1)} %get-tuple-element.96) | copy-start | bytes 9220
  43.7 88.2 %copy-start.30 = (f32[16,48]{1,0:T(8,128)}, f32[16,48]{1,0:T(8,128)S(1)}, u32[]{:S(2)}) copy-start(f32[16,48]{1,0:T(8,128)S(1)} %get-tuple-element.79) | copy-start | bytes 9220
  43.7 88.2 %copy-start.32 = (f32[16,48]{1,0:T(8,128)}, f32[16,48]{1,0:T(8,128)S(1)}, u32[]{:S(2)}) copy-start(f32[16,48]{1,0:T(8,128)S(1)} %get-tuple-element.80) | copy-start | bytes 9220
  43.8 88.2 %copy-start.34 = (f32[16,48]{1,0:T(8,128)}, f32[16,48]{1,0:T(8,128)S(1)}, u32[]{:S(2)}) copy-start(f32[16,48]{1,0:T(8,128)S(1)} %get-tuple-element.81) | copy-start | bytes 9220
  179.7 421.8 %copy-start.72 = (s32[2048]{0:T(1024)S(1)}, s32[2048]{0:T(1024)}, u32[]{:S(2)}) copy-start(s32[2048]{0:T(1024)} %param.11) | copy-start | bytes 24580
  179.7 467.5 %copy-start.43 = (f32[16,48]{1,0:T(8,128)S(1)}, f32[16,48]{1,0:T(8,128)}, u32[]{:S(2)}) copy-start(f32[16,48]{1,0:T(8,128)} %copy-done.42) | copy-start | bytes 9220
  539.6 7.9 collective-permute-start.30
  540.9 5.2 collective-permute-start.31
  542.2 6.6 collective-permute-start.29
  543.5 6.6 collective-permute-start.28
  544.9 7.2 collective-permute-start.27
  546.2 21.1 %collective-permute-start.26 = (f32[16,3072]{1,0:T(8,128)S(1)}, f32[16,3072]{1,0:T(8,128)S(1)}, u32[]{:S(2)}, u32[]{:S(2)}) collective-permute-start(f32[16,3072]{1,0:T(8,128)S(1)} %fusion), channel_id=1, source_target_pairs={{0,27},{1,28},{2,29},{3,30},{4,31},{5,32},{6,33},{7,34},{8,35},{9,... | collective-permute-start | bytes 589832
  547.5 26.2 %collective-permute-start.25 = (f32[16,3072]{1,0:T(8,128)S(1)}, f32[16,3072]{1,0:T(8,128)S(1)}, u32[]{:S(2)}, u32[]{:S(2)}) collective-permute-start(f32[16,3072]{1,0:T(8,128)S(1)} %fusion), channel_id=1, source_target_pairs={{0,26},{1,27},{2,28},{3,29},{4,30},{5,31},{6,32},{7,33},{8,34},{9,... | collective-permute-start | bytes 589832
  548.8 30.6 %collective-permute-start.24 = (f32[16,3072]{1,0:T(8,128)S(1)}, f32[16,3072]{1,0:T(8,128)S(1)}, u32[]{:S(2)}, u32[]{:S(2)}) collective-permute-start(f32[16,3072]{1,0:T(8,128)S(1)} %fusion), channel_id=1, source_target_pairs={{0,25},{1,26},{2,27},{3,28},{4,29},{5,30},{6,31},{7,32},{8,33},{9,... | collective-permute-start | bytes 589832
  550.2 37.6 %collective-permute-start.23 = (f32[16,3072]{1,0:T(8,128)S(1)}, f32[16,3072]{1,0:T(8,128)S(1)}, u32[]{:S(2)}, u32[]{:S(2)}) collective-permute-start(f32[16,3072]{1,0:T(8,128)S(1)} %fusion), channel_id=1, source_target_pairs={{0,24},{1,25},{2,26},{3,27},{4,28},{5,29},{6,30},{7,31},{8,32},{9,... | collective-permute-start | bytes 589832
  552.0 37.8 %collective-permute-start.22 = (f32[16,3072]{1,0:T(8,128)S(1)}, f32[16,3072]{1,0:T(8,128)S(1)}, u32[]{:S(2)}, u32[]{:S(2)}) collective-permute-start(f32[16,3072]{1,0:T(8,128)S(1)} %fusion), channel_id=1, source_target_pairs={{0,23},{1,24},{2,25},{3,26},{4,27},{5,28},{6,29},{7,30},{8,31},{9,... | collective-permute-start | bytes 589832
  567.3 28.4 %collective-permute-start.21 = (f32[16,3072]{1,0:T(8,128)S(1)}, f32[16,3072]{1,0:T(8,128)S(1)}, u32[]{:S(2)}, u32[]{:S(2)}) collective-permute-start(f32[16,3072]{1,0:T(8,128)S(1)} %fusion), channel_id=1, source_target_pairs={{0,22},{1,23},{2,24},{3,25},{4,26},{5,27},{6,28},{7,29},{8,30},{9,... | collective-permute-start | bytes 589832
  573.7 24.0 %collective-permute-start.20 = (f32[16,3072]{1,0:T(8,128)S(1)}, f32[16,3072]{1,0:T(8,128)S(1)}, u32[]{:S(2)}, u32[]{:S(2)}) collective-permute-start(f32[16,3072]{1,0:T(8,128)S(1)} %fusion), channel_id=1, source_target_pairs={{0,21},{1,22},{2,23},{3,24},{4,25},{5,26},{6,27},{7,28},{8,29},{9,... | collective-permute-start | bytes 589832
  579.4 23.7 %collective-permute-start.19 = (f32[16,3072]{1,0:T(8,128)S(1)}, f32[16,3072]{1,0:T(8,128)}, u32[]{:S(2)}, u32[]{:S(2)}) collective-permute-start(f32[16,3072]{1,0:T(8,128)S(1)} %fusion), channel_id=1, source_target_pairs={{0,20},{1,21},{2,22},{3,23},{4,24},{5,25},{6,26},{7,27},{8,28},{9,... | collective-permute-start | bytes 589832
  587.8 20.8 %collective-permute-start.18 = (f32[16,3072]{1,0:T(8,128)S(1)}, f32[16,3072]{1,0:T(8,128)}, u32[]{:S(2)}, u32[]{:S(2)}) collective-permute-start(f32[16,3072]{1,0:T(8,128)S(1)} %fusion), channel_id=1, source_target_pairs={{0,19},{1,20},{2,21},{3,22},{4,23},{5,24},{6,25},{7,26},{8,27},{9,... | collective-permute-start | bytes 589832
  589.8 31.1 %collective-permute-start.17 = (f32[16,3072]{1,0:T(8,128)S(1)}, f32[16,3072]{1,0:T(8,128)}, u32[]{:S(2)}, u32[]{:S(2)}) collective-permute-start(f32[16,3072]{1,0:T(8,128)S(1)} %fusion), channel_id=1, source_target_pairs={{0,18},{1,19},{2,20},{3,21},{4,22},{5,23},{6,24},{7,25},{8,26},{9,... | collective-permute-start | bytes 589832
  595.7 35.5 %collective-permute-start.16 = (f32[16,3072]{1,0:T(8,128)S(1)}, f32[16,3072]{1,0:T(8,128)}, u32[]{:S(2)}, u32[]{:S(2)}) collective-permute-start(f32[16,3072]{1,0:T(8,128)S(1)} %fusion), channel_id=1, source_target_pairs={{0,17},{1,18},{2,19},{3,20},{4,21},{5,22},{6,23},{7,24},{8,25},{9,... | collective-permute-start | bytes 589832
  597.7 48.2 %collective-permute-start.15 = (f32[16,3072]{1,0:T(8,128)S(1)}, f32[16,3072]{1,0:T(8,128)}, u32[]{:S(2)}, u32[]{:S(2)}) collective-permute-start(f32[16,3072]{1,0:T(8,128)S(1)} %fusion), channel_id=1, source_target_pairs={{0,16},{1,17},{2,18},{3,19},{4,20},{5,21},{6,22},{7,23},{8,24},{9,... | collective-permute-start | bytes 589832
  603.1 70.1 %collective-permute-start.14 = (f32[16,3072]{1,0:T(8,128)S(1)}, f32[16,3072]{1,0:T(8,128)S(1)}, u32[]{:S(2)}, u32[]{:S(2)}) collective-permute-start(f32[16,3072]{1,0:T(8,128)S(1)} %fusion), channel_id=1, source_target_pairs={{0,15},{1,16},{2,17},{3,18},{4,19},{5,20},{6,21},{7,22},{8,23},{9,... | collective-permute-start | bytes 589832
  608.6 65.9 %collective-permute-start.13 = (f32[16,3072]{1,0:T(8,128)S(1)}, f32[16,3072]{1,0:T(8,128)S(1)}, u32[]{:S(2)}, u32[]{:S(2)}) collective-permute-start(f32[16,3072]{1,0:T(8,128)S(1)} %fusion), channel_id=1, source_target_pairs={{0,14},{1,15},{2,16},{3,17},{4,18},{5,19},{6,20},{7,21},{8,22},{9,... | collective-permute-start | bytes 589832
  620.9 58.9 %collective-permute-start.12 = (f32[16,3072]{1,0:T(8,128)S(1)}, f32[16,3072]{1,0:T(8,128)S(1)}, u32[]{:S(2)}, u32[]{:S(2)}) collective-permute-start(f32[16,3072]{1,0:T(8,128)S(1)} %fusion), channel_id=1, source_target_pairs={{0,13},{1,14},{2,15},{3,16},{4,17},{5,18},{6,19},{7,20},{8,21},{9,... | collective-permute-start | bytes 589832
  631.2 50.6 %collective-permute-start.11 = (f32[16,3072]{1,0:T(8,128)S(1)}, f32[16,3072]{1,0:T(8,128)S(1)}, u32[]{:S(2)}, u32[]{:S(2)}) collective-permute-start(f32[16,3072]{1,0:T(8,128)S(1)} %fusion), channel_id=1, source_target_pairs={{0,12},{1,13},{2,14},{3,15},{4,16},{5,17},{6,18},{7,19},{8,20},{9,... | collective-permute-start | bytes 589832
  646.0 38.4 %collective-permute-start.10 = (f32[16,3072]{1,0:T(8,128)S(1)}, f32[16,3072]{1,0:T(8,128)S(1)}, u32[]{:S(2)}, u32[]{:S(2)}) collective-permute-start(f32[16,3072]{1,0:T(8,128)S(1)} %fusion), channel_id=1, source_target_pairs={{0,11},{1,12},{2,13},{3,14},{4,15},{5,16},{6,17},{7,18},{8,19},{9,... | collective-permute-start | bytes 589832
  673.3 23.7 %collective-permute-start.9 = (f32[16,3072]{1,0:T(8,128)S(1)}, f32[16,3072]{1,0:T(8,128)S(1)}, u32[]{:S(2)}, u32[]{:S(2)}) collective-permute-start(f32[16,3072]{1,0:T(8,128)S(1)} %fusion), channel_id=1, source_target_pairs={{0,10},{1,11},{2,12},{3,13},{4,14},{5,15},{6,16},{7,17},{8,18},{9,... | collective-permute-start | bytes 589832
  674.6 29.1 %collective-permute-start.8 = (f32[16,3072]{1,0:T(8,128)S(1)}, f32[16,3072]{1,0:T(8,128)S(1)}, u32[]{:S(2)}, u32[]{:S(2)}) collective-permute-start(f32[16,3072]{1,0:T(8,128)S(1)} %fusion), channel_id=1, source_target_pairs={{0,9},{1,10},{2,11},{3,12},{4,13},{5,14},{6,15},{7,16},{8,17},{9,1... | collective-permute-start | bytes 589832
  679.9 25.8 %collective-permute-start.7 = (f32[16,3072]{1,0:T(8,128)S(1)}, f32[16,3072]{1,0:T(8,128)S(1)}, u32[]{:S(2)}, u32[]{:S(2)}) collective-permute-start(f32[16,3072]{1,0:T(8,128)S(1)} %fusion), channel_id=1, source_target_pairs={{0,8},{1,9},{2,10},{3,11},{4,12},{5,13},{6,14},{7,15},{8,16},{9,17... | collective-permute-start | bytes 589832
  681.8 28.5 %collective-permute-start.6 = (f32[16,3072]{1,0:T(8,128)S(1)}, f32[16,3072]{1,0:T(8,128)S(1)}, u32[]{:S(2)}, u32[]{:S(2)}) collective-permute-start(f32[16,3072]{1,0:T(8,128)S(1)} %fusion), channel_id=1, source_target_pairs={{0,7},{1,8},{2,9},{3,10},{4,11},{5,12},{6,13},{7,14},{8,15},{9,16}... | collective-permute-start | bytes 589832
  685.1 27.1 %collective-permute-start.5 = (f32[16,3072]{1,0:T(8,128)S(1)}, f32[16,3072]{1,0:T(8,128)S(1)}, u32[]{:S(2)}, u32[]{:S(2)}) collective-permute-start(f32[16,3072]{1,0:T(8,128)S(1)} %fusion), channel_id=1, source_target_pairs={{0,6},{1,7},{2,8},{3,9},{4,10},{5,11},{6,12},{7,13},{8,14},{9,15},... | collective-permute-start | bytes 589832
  697.0 25.4 %collective-permute-start.4 = (f32[16,3072]{1,0:T(8,128)S(1)}, f32[16,3072]{1,0:T(8,128)}, u32[]{:S(2)}, u32[]{:S(2)}) collective-permute-start(f32[16,3072]{1,0:T(8,128)S(1)} %fusion), channel_id=1, source_target_pairs={{0,5},{1,6},{2,7},{3,8},{4,9},{5,10},{6,11},{7,12},{8,13},{9,14},{... | collective-permute-start | bytes 589832
  703.7 18.6 %collective-permute-start.3 = (f32[16,3072]{1,0:T(8,128)S(1)}, f32[16,3072]{1,0:T(8,128)}, u32[]{:S(2)}, u32[]{:S(2)}) collective-permute-start(f32[16,3072]{1,0:T(8,128)S(1)} %fusion), channel_id=1, source_target_pairs={{0,4},{1,5},{2,6},{3,7},{4,8},{5,9},{6,10},{7,11},{8,12},{9,13},{1... | collective-permute-start | bytes 589832
  705.7 16.7 %collective-permute-start.2 = (f32[16,3072]{1,0:T(8,128)S(1)}, f32[16,3072]{1,0:T(8,128)}, u32[]{:S(2)}, u32[]{:S(2)}) collective-permute-start(f32[16,3072]{1,0:T(8,128)S(1)} %fusion), channel_id=1, source_target_pairs={{0,3},{1,4},{2,5},{3,6},{4,7},{5,8},{6,9},{7,10},{8,11},{9,12},{10... | collective-permute-start | bytes 589832
  710.3 12.1 %collective-permute-start.1 = (f32[16,3072]{1,0:T(8,128)S(1)}, f32[16,3072]{1,0:T(8,128)}, u32[]{:S(2)}, u32[]{:S(2)}) collective-permute-start(f32[16,3072]{1,0:T(8,128)S(1)} %fusion), channel_id=1, source_target_pairs={{0,2},{1,3},{2,4},{3,5},{4,6},{5,7},{6,8},{7,9},{8,10},{9,11},{10,... | collective-permute-start | bytes 589832
  712.9 9.5 %collective-permute-start = (f32[16,3072]{1,0:T(8,128)S(1)}, f32[16,3072]{1,0:T(8,128)}, u32[]{:S(2)}, u32[]{:S(2)}) collective-permute-start(f32[16,3072]{1,0:T(8,128)S(1)} %fusion), channel_id=1, source_target_pairs={{0,1},{1,2},{2,3},{3,4},{4,5},{5,6},{6,7},{7,8},{8,9},{9,10},{10,1... | collective-permute-start | bytes 589832
  722.3 187.8 %all-gather.6.cloned.1.call-start = ((), (), s32[]{:S(2)}) async-start(), calls=%async_computation.2 | async-start | bytes 3342336 | tf_op jit(solution)/shard_map/all_gather | solution.py:111
  (62 other events, 2134.4 us)
Sparse Core Ops, SparseCore 0:
  9.7 57.9 all-gather.3
  722.4 139.3 all-reduce.6
  864.2 45.8 all-gather.5
where the time goes:
time: 927 us; the launch traced here: 924 us
  blocking collectives  424 us (46%)
  other arithmetic  145 us (16%)
  starting transfers between devices  136 us (15%)
  local copies, waits for them, and re-layouts  128 us (14%)
  waiting for transfers between devices  38.2 us (4%)
  matrix products  35.9 us (4%)
  between operations  16.2 us (2%)
    unnamed x1, blocking collectives  360 us
    unnamed x32, starting transfers between devices  136 us
    unnamed x153, local copies, waits for them, and re-layouts  92.8 us
    reduce_sum x4, other arithmetic, block_pass(): kernel_terms.append(jnp.sum(grad_conv * window * same_seg, axis=(0, 1)))  88.1 us
    psum x1, blocking collectives, local(): kernel_total, gain_total = lax.psum((kernel_part, gain_part), ('dp', 'red'))  63.9 us
    another operation x2, other arithmetic  35.5 us
    all_gather x1, waiting for transfers between devices, local(): weights = lax.all_gather(w_in, 'red', axis=0, tiled=True)  23.9 us
  transfers between devices with their start and end apart: 35, of which 3 were waited for; matrix products, arithmetic and copies ran while one was open for 20% of the time, Pallas kernels for 0%

commit v1 on v0

--- a/solution.py
+++ b/solution.py
@@ -85,7 +85,9 @@
     dp_index = lax.axis_index("dp")
     red_index = lax.axis_index("red")
     local_utts, length, model_width = frames.shape
-    weights = lax.all_gather(w_in, "red", axis=0, tiled=True)
+    weights = jnp.concatenate(
+        lax.all_to_all(jnp.stack([w_in] * lax.axis_size("red")), "red", 0, 0), axis=0
+    )
     positions = jnp.arange(length, dtype=jnp.int32)
     by_owner = lengths.reshape(dp_size, red_size, local_utts)
     own_lengths = lax.dynamic_slice(by_owner, (dp_index, red_index, 0), (1, 1, local_utts)).reshape(

time: 927 us -> 968 us (1.044)
  waiting for transfers between devices: 38.2 us -> 83.4 us
    all_to_all x0 -> x1, waiting for transfers between devices: none -> 72.3 us  [local(): lax.all_to_all(jnp.stack([w_in] * lax.axis_size('red')), 'red', 0, 0)]
    all_gather x1 -> x0, waiting for transfers between devices: 23.9 us -> none  [local(): weights = lax.all_gather(w_in, 'red', axis=0, tiled=True)]
    all_gather x1, waiting for transfers between devices: 12.9 us -> 0.01 us  [local(): grad_weights = lax.all_gather(owned_rows, 'dp', axis=0, tiled=True)]
    unnamed x32, starting transfers between devices: 136 us -> 125 us
    unnamed x35 -> x34, waiting for transfers between devices: 1.34 us -> 11.1 us
    unnamed x153 -> x131, local copies, waits for them, and re-layouts: 92.8 us -> 92.7 us
  transfers between devices with their start and end apart: 35 -> 35, of which waited for: 3 -> 3; matrix products, arithmetic and copies ran while one was open for 20% -> 19% of each run, Pallas kernels for 0% -> 0%
where the time goes in v1:
time: 968 us; the launch traced here: 964 us
  blocking collectives  424 us (44%)
  other arithmetic  139 us (14%)
  local copies, waits for them, and re-layouts  132 us (14%)
  starting transfers between devices  132 us (14%)
  waiting for transfers between devices  83.4 us (9%)
  matrix products  35.9 us (4%)
  between operations  17.7 us (2%)
    unnamed x1, blocking collectives  360 us
    unnamed x32, starting transfers between devices  125 us
    unnamed x131, local copies, waits for them, and re-layouts  92.7 us
    reduce_sum x4, other arithmetic, block_pass(): kernel_terms.append(jnp.sum(grad_conv * window * same_seg, axis=(0, 1)))  87.3 us
    all_to_all x1, waiting for transfers between devices, local(): lax.all_to_all(jnp.stack([w_in] * lax.axis_size('red')), 'red', 0, 0)  72.3 us
    psum x1, blocking collectives, local(): kernel_total, gain_total = lax.psum((kernel_part, gain_part), ('dp', 'red'))  63.9 us
    another operation x2, other arithmetic  34.1 us
  transfers between devices with their start and end apart: 35, of which 3 were waited for; matrix products, arithmetic and copies ran while one was open for 19% of the time, Pallas kernels for 0%

profile of v1, /device:TPU:1, one launch (start us, length us, event | category | flops | bytes accessed | tf_op | source)
XLA Modules:
  0.0 963.9 jit_solution(3489634678133733957)
XLA Ops:
  8.0 6.1 stack.107
  14.1 6.9 all-to-all-start
  22.9 2.2 fusion.7
  25.1 8.3 copy.13
  33.4 10.5 %reshape_reshape.3 = bf16[768,8,16,12]{0,3,2,1:T(8,128)(2,1)} reshape(bf16[16,48,1536]{1,0,2:T(8,128)(2,1)} %copy.13) | data formatting | bytes 4718592 | tf_op jit(solution)/shard_map/reshape;reshape | solution.py:103
  43.9 3.9 copy.14
  47.8 4.9 reshape.145
  53.8 72.3 %all-to-all-done = bf16[8,192,3072]{2,1,0:T(8,128)(2,1)} async-done(((bf16[8,192,3072]{2,1,0:T(8,128)(2,1)}), bf16[8,192,3072]{2,1,0:T(8,128)(2,1)}, u32[]{:S(2)}, u32[]{:S(2)}) %all-to-all-start) | async-done | bytes 9437216 | tf_op jit(solution)/shard_map/all_to_all | solution.py:89
  126.1 10.8 %fusion.155 = f32[16,48,3072]{2,1,0:T(8,128)S(1)} fusion(bf16[16,48,1536]{2,1,0:T(8,128)(2,1)} %fusion.7, bf16[1536,3072,1]{1,0,2:T(8,128)(2,1)} %bitcast.1), kind=kOutput, calls=%fused_computation.327 | convolution fusion | flops 7247757312 | bytes 21233664 | tf_op jit(solution)/shard_map/dot_general | solution.py:23
  138.3 2.7 copy-done.3
  140.9 48.5 %multiply_reduce_fusion = (f32[1536]{0:T(1024)}, f32[1536]{0:T(1024)}, f32[1536]{0:T(1024)}, f32[1536]{0:T(1024)}, f32[1536]{0:T(1024)}, /*index=5*/f32[1536]{0:...) fusion(f32[16,48,1536]{2,1,0:T(8,128)S(1)} %multiply_multiply_f, ...), kind=kLoop, calls=%fused_computation.183 | loop fusion | flops 150981120 | bytes 16856064 | tf_op jit(solution)/shard_map/reduce_sum | solution.py:50
  189.5 27.9 %multiply_convert_fusion.1 = (bf16[16,48,1536]{2,1,0:T(8,128)(2,1)}, f32[16,48,1536]{2,1,0:T(8,128)}) fusion(f32[16,48,3072]{2,1,0:T(8,128)} %copy-done.3, f32[16,48]{1,0:T(8,128)S(1)} %get-tuple-element.106, f32[16,48]{1,0:T(8,128)S(1)} %get-tuple-element.76, f32[1536]{0:T(1024)S(1)} %get-tuple-element.68, f32[16,48]{1,0:T(8,128)S(1)} %get-tuple-element.77, ...), kind=kLoop, calls=%fused_computation.215 | loop fusion | flops 114425856 | bytes 16800768 | tf_op jit(solution)/shard_map/convert.4
  217.4 6.2 multiply_convert_fusion
  225.0 10.8 %fusion.116 = f32[1536,3072]{1,0:T(8,128)} fusion(bf16[768,1536]{0,1:T(8,128)(2,1)S(1)} %copy-done.8, bf16[768,1536]{1,0:T(8,128)(2,1)S(1)} %bitcast.22, bf16[768,1536]{1,0:T(8,128)(2,1)S(1)} %bitcast.21), kind=kOutput, calls=%fused_computation.179 | convolution fusion | flops 7257194496 | bytes 25952256 | tf_op jit(solution)/shard_map/dot_general | solution.py:106
  235.9 360.4 %fusion = f32[16,3072]{1,0:T(8,128)S(1)} fusion(f32[1536,3072]{1,0:T(8,128)} %fusion.116), kind=kCustom, calls=%all-reduce-scatter | all-reduce-scatter fusion | flops 6291457 | bytes 19070976
  608.1 3.0 collective-permute-done.27
  611.1 12.0 %collective-permute-start.22 = (f32[16,3072]{1,0:T(8,128)S(1)}, f32[16,3072]{1,0:T(8,128)S(1)}, u32[]{:S(2)}, u32[]{:S(2)}) collective-permute-start(f32[16,3072]{1,0:T(8,128)S(1)} %fusion), channel_id=1, source_target_pairs={{0,23},{1,24},{2,25},{3,26},{4,27},{5,28},{6,29},{7,30},{8,31},{9,... | collective-permute-start | bytes 589832
  623.1 6.4 collective-permute-start.21
  629.5 5.7 collective-permute-start.20
  635.2 8.4 collective-permute-start.19
  643.6 2.0 collective-permute-start.18
  645.6 8.1 collective-permute-done.22
  653.6 2.0 collective-permute-start.17
  655.6 2.0 collective-permute-start.16
  657.6 2.0 collective-permute-start.15
  661.2 3.3 collective-permute-start.14
  664.5 12.1 %collective-permute-start.13 = (f32[16,3072]{1,0:T(8,128)S(1)}, f32[16,3072]{1,0:T(8,128)S(1)}, u32[]{:S(2)}, u32[]{:S(2)}) collective-permute-start(f32[16,3072]{1,0:T(8,128)S(1)} %fusion), channel_id=1, source_target_pairs={{0,14},{1,15},{2,16},{3,17},{4,18},{5,19},{6,20},{7,21},{8,22},{9,... | collective-permute-start | bytes 589832
  676.7 10.3 %collective-permute-start.12 = (f32[16,3072]{1,0:T(8,128)S(1)}, f32[16,3072]{1,0:T(8,128)S(1)}, u32[]{:S(2)}, u32[]{:S(2)}) collective-permute-start(f32[16,3072]{1,0:T(8,128)S(1)} %fusion), channel_id=1, source_target_pairs={{0,13},{1,14},{2,15},{3,16},{4,17},{5,18},{6,19},{7,20},{8,21},{9,... | collective-permute-start | bytes 589832
  687.0 14.7 %collective-permute-start.11 = (f32[16,3072]{1,0:T(8,128)S(1)}, f32[16,3072]{1,0:T(8,128)S(1)}, u32[]{:S(2)}, u32[]{:S(2)}) collective-permute-start(f32[16,3072]{1,0:T(8,128)S(1)} %fusion), channel_id=1, source_target_pairs={{0,12},{1,13},{2,14},{3,15},{4,16},{5,17},{6,18},{7,19},{8,20},{9,... | collective-permute-start | bytes 589832
  703.0 25.9 %multiply_reduce_fusion.9 = (f32[1536]{0:T(1024)S(1)}, f32[1536]{0:T(1024)S(1)}, f32[1536]{0:T(1024)S(1)}, f32[1536]{0:T(1024)S(1)}, f32[1536]{0:T(1024)S(1)}, /...) fusion(f32[16,48,1536]{2,1,0:T(8,128)} %copy-done.1, f32[16,48,1536]{2,1,0:T(8,128)} %copy-done, ...), kind=kLoop, calls=%fused_computation.192 | loop fusion | flops 30657024 | bytes 9517056 | tf_op jit(solution)/shard_map/reduce_sum | solution.py:50
  730.3 5.2 collective-permute-start.8
  735.5 1.9 collective-permute-start.7
  737.5 2.5 collective-permute-start.6
  740.8 2.7 collective-permute-start.5
  743.6 9.0 multiply_reduce_fusion.18
  752.7 6.7 collective-permute-start.4
  759.4 2.0 collective-permute-start.3
  761.4 4.6 collective-permute-start.2
  765.9 2.0 collective-permute-start.1
  768.6 2.1 collective-permute-start
  770.7 3.9 multiply_reduce_fusion.27
  775.2 2.7 stack.139
  778.1 84.8 %concatenate.17 = f32[524,3072]{1,0:T(8,128)} concatenate(f32[12,3072]{1,0:T(8,128)S(1)} %collective-permute-done.31, f32[16,3072]{1,0:T(8,128)S(1)} %collective-permute-done.30, f32[16,3072]{1,0:T(8,128)} %copy-done.9, f32[16,3072]{1,0:T(8,128)} %copy-done.10, f32[16,3072]{1,0:T(8,128)} %copy-done.11, f32[16,3072]{1,0:T(8,128)} %copy-done.12, f32[16,3072]{1,0:T(8,128)} %copy-done.13, ...), dimensions={0} | concatenate | bytes 12877824
  862.9 1.7 dynamic-slice_bitcast_fusion
  864.6 14.3 %fusion.14 = (f32[1536]{0:T(1024)S(1)}, f32[16,48]{1,0:T(8,128)S(1)}, f32[16,48]{1,0:T(8,128)S(1)}, f32[16,48,1536]{2,1,0:T(8,128)}) fusion(bf16[16,48,1536]{2,1,0:T(8,128)(2,1)S(1)} %copy-done.4, f32[16,48]{1,0:T(8,128)S(1)} %copy-done.49, f32[16,48]{1,0:T(8,128)S(1)} %copy-done.47, f32[1536]{0:T(1024)S(1)} %copy-done.51, ...), kind=kOutput, calls=%fused_computation.76 | convolution fusion | flops 7267808256 | bytes 21258240 | tf_op jit(solution)/shard_map/dot_general | solution.py:67
  878.9 63.9 %psum.15 = f32[1536]{0:T(1024)S(1)} all-reduce(f32[1536]{0:T(1024)S(1)} %get-tuple-element.36), channel_id=1, replica_groups=mesh['dp'=16,'red'=8] {'dp','red'}, use_global_device_ids=true, to_apply=%region_39.40 | all-reduce | flops 1536 | bytes 12288 | tf_op jit(solution)/shard_map/psum | solution.py:114
  943.3 7.8 fusion.13
  952.8 2.1 broadcast_multiply_fusion
  (226 shorter events, 26.3 us)
Async XLA Ops:
  14.1 112.0 %all-to-all-start = ((bf16[8,192,3072]{2,1,0:T(8,128)(2,1)}), bf16[8,192,3072]{2,1,0:T(8,128)(2,1)}, u32[]{:S(2)}, u32[]{:S(2)}) async-start(bf16[8,192,3072]{2,1,0:T(8,128)(2,1)} %stack.107), calls=%async_computation | async-start | bytes 18874368 | tf_op jit(solution)/shard_map/all_to_all | solution.py:89
  21.0 930.1 %all-reduce.7.cloned.1.call-start = ((), (), s32[]{:S(2)}) async-start(), calls=%async_computation.1 | async-start | bytes 393216 | tf_op jit(solution)/shard_map/psum | solution.py:114
  53.5 135.9 %copy-start.38 = (f32[16,48]{1,0:T(8,128)}, f32[16,48]{1,0:T(8,128)S(1)}, u32[]{:S(2)}) copy-start(f32[16,48]{1,0:T(8,128)S(1)} %get-tuple-element.89) | copy-start | bytes 9220
  53.5 135.9 %copy-start.39 = (f32[16,48]{1,0:T(8,128)}, f32[16,48]{1,0:T(8,128)S(1)}, u32[]{:S(2)}) copy-start(f32[16,48]{1,0:T(8,128)S(1)} %get-tuple-element.90) | copy-start | bytes 9220
  53.5 135.9 %copy-start.40 = (f32[16,48]{1,0:T(8,128)}, f32[16,48]{1,0:T(8,128)S(1)}, u32[]{:S(2)}) copy-start(f32[16,48]{1,0:T(8,128)S(1)} %get-tuple-element.91) | copy-start | bytes 9220
  53.6 135.9 %copy-start.41 = (f32[16,48]{1,0:T(8,128)}, f32[16,48]{1,0:T(8,128)S(1)}, u32[]{:S(2)}) copy-start(f32[16,48]{1,0:T(8,128)S(1)} %get-tuple-element.92) | copy-start | bytes 9220
  53.6 135.9 %copy-start.42 = (f32[16,48]{1,0:T(8,128)}, f32[16,48]{1,0:T(8,128)S(1)}, u32[]{:S(2)}) copy-start(f32[16,48]{1,0:T(8,128)S(1)} %get-tuple-element.93) | copy-start | bytes 9220
  53.7 135.8 %copy-start.43 = (f32[16,48]{1,0:T(8,128)}, f32[16,48]{1,0:T(8,128)S(1)}, u32[]{:S(2)}) copy-start(f32[16,48]{1,0:T(8,128)S(1)} %get-tuple-element.94) | copy-start | bytes 9220
  53.7 135.8 %copy-start.44 = (f32[16,48]{1,0:T(8,128)}, f32[16,48]{1,0:T(8,128)S(1)}, u32[]{:S(2)}) copy-start(f32[16,48]{1,0:T(8,128)S(1)} %get-tuple-element.95) | copy-start | bytes 9220
  53.7 135.8 %copy-start.45 = (f32[16,48]{1,0:T(8,128)}, f32[16,48]{1,0:T(8,128)S(1)}, u32[]{:S(2)}) copy-start(f32[16,48]{1,0:T(8,128)S(1)} %get-tuple-element.96) | copy-start | bytes 9220
  53.8 135.7 %copy-start.30 = (f32[16,48]{1,0:T(8,128)}, f32[16,48]{1,0:T(8,128)S(1)}, u32[]{:S(2)}) copy-start(f32[16,48]{1,0:T(8,128)S(1)} %get-tuple-element.81) | copy-start | bytes 9220
  53.8 135.7 %copy-start.32 = (f32[16,48]{1,0:T(8,128)}, f32[16,48]{1,0:T(8,128)S(1)}, u32[]{:S(2)}) copy-start(f32[16,48]{1,0:T(8,128)S(1)} %get-tuple-element.82) | copy-start | bytes 9220
  53.8 135.7 %copy-start.34 = (f32[16,48]{1,0:T(8,128)}, f32[16,48]{1,0:T(8,128)S(1)}, u32[]{:S(2)}) copy-start(f32[16,48]{1,0:T(8,128)S(1)} %get-tuple-element.83) | copy-start | bytes 9220
  53.8 135.7 %copy-start.36 = (f32[16,48]{1,0:T(8,128)}, f32[16,48]{1,0:T(8,128)S(1)}, u32[]{:S(2)}) copy-start(f32[16,48]{1,0:T(8,128)S(1)} %get-tuple-element.84) | copy-start | bytes 9220
  596.2 7.9 collective-permute-start.30
  597.6 5.2 collective-permute-start.31
  598.9 6.6 collective-permute-start.29
  600.2 6.6 collective-permute-start.28
  601.5 9.6 collective-permute-start.27
  602.8 20.3 %collective-permute-start.26 = (f32[16,3072]{1,0:T(8,128)S(1)}, f32[16,3072]{1,0:T(8,128)S(1)}, u32[]{:S(2)}, u32[]{:S(2)}) collective-permute-start(f32[16,3072]{1,0:T(8,128)S(1)} %fusion), channel_id=1, source_target_pairs={{0,27},{1,28},{2,29},{3,30},{4,31},{5,32},{6,33},{7,34},{8,35},{9,... | collective-permute-start | bytes 589832
  604.1 25.3 %collective-permute-start.25 = (f32[16,3072]{1,0:T(8,128)S(1)}, f32[16,3072]{1,0:T(8,128)S(1)}, u32[]{:S(2)}, u32[]{:S(2)}) collective-permute-start(f32[16,3072]{1,0:T(8,128)S(1)} %fusion), channel_id=1, source_target_pairs={{0,26},{1,27},{2,28},{3,29},{4,30},{5,31},{6,32},{7,33},{8,34},{9,... | collective-permute-start | bytes 589832
  605.5 29.7 %collective-permute-start.24 = (f32[16,3072]{1,0:T(8,128)S(1)}, f32[16,3072]{1,0:T(8,128)S(1)}, u32[]{:S(2)}, u32[]{:S(2)}) collective-permute-start(f32[16,3072]{1,0:T(8,128)S(1)} %fusion), channel_id=1, source_target_pairs={{0,25},{1,26},{2,27},{3,28},{4,29},{5,30},{6,31},{7,32},{8,33},{9,... | collective-permute-start | bytes 589832
  606.8 36.8 %collective-permute-start.23 = (f32[16,3072]{1,0:T(8,128)S(1)}, f32[16,3072]{1,0:T(8,128)S(1)}, u32[]{:S(2)}, u32[]{:S(2)}) collective-permute-start(f32[16,3072]{1,0:T(8,128)S(1)} %fusion), channel_id=1, source_target_pairs={{0,24},{1,25},{2,26},{3,27},{4,28},{5,29},{6,30},{7,31},{8,32},{9,... | collective-permute-start | bytes 589832
  611.1 42.6 %collective-permute-start.22 = (f32[16,3072]{1,0:T(8,128)S(1)}, f32[16,3072]{1,0:T(8,128)S(1)}, u32[]{:S(2)}, u32[]{:S(2)}) collective-permute-start(f32[16,3072]{1,0:T(8,128)S(1)} %fusion), channel_id=1, source_target_pairs={{0,23},{1,24},{2,25},{3,26},{4,27},{5,28},{6,29},{7,30},{8,31},{9,... | collective-permute-start | bytes 589832
  623.1 32.5 %collective-permute-start.21 = (f32[16,3072]{1,0:T(8,128)S(1)}, f32[16,3072]{1,0:T(8,128)S(1)}, u32[]{:S(2)}, u32[]{:S(2)}) collective-permute-start(f32[16,3072]{1,0:T(8,128)S(1)} %fusion), channel_id=1, source_target_pairs={{0,22},{1,23},{2,24},{3,25},{4,26},{5,27},{6,28},{7,29},{8,30},{9,... | collective-permute-start | bytes 589832
  629.5 28.1 %collective-permute-start.20 = (f32[16,3072]{1,0:T(8,128)S(1)}, f32[16,3072]{1,0:T(8,128)S(1)}, u32[]{:S(2)}, u32[]{:S(2)}) collective-permute-start(f32[16,3072]{1,0:T(8,128)S(1)} %fusion), channel_id=1, source_target_pairs={{0,21},{1,22},{2,23},{3,24},{4,25},{5,26},{6,27},{7,28},{8,29},{9,... | collective-permute-start | bytes 589832
  635.2 25.9 %collective-permute-start.19 = (f32[16,3072]{1,0:T(8,128)S(1)}, f32[16,3072]{1,0:T(8,128)}, u32[]{:S(2)}, u32[]{:S(2)}) collective-permute-start(f32[16,3072]{1,0:T(8,128)S(1)} %fusion), channel_id=1, source_target_pairs={{0,20},{1,21},{2,22},{3,23},{4,24},{5,25},{6,26},{7,27},{8,28},{9,... | collective-permute-start | bytes 589832
  643.6 20.9 %collective-permute-start.18 = (f32[16,3072]{1,0:T(8,128)S(1)}, f32[16,3072]{1,0:T(8,128)}, u32[]{:S(2)}, u32[]{:S(2)}) collective-permute-start(f32[16,3072]{1,0:T(8,128)S(1)} %fusion), channel_id=1, source_target_pairs={{0,19},{1,20},{2,21},{3,22},{4,23},{5,24},{6,25},{7,26},{8,27},{9,... | collective-permute-start | bytes 589832
  653.6 23.0 %collective-permute-start.17 = (f32[16,3072]{1,0:T(8,128)S(1)}, f32[16,3072]{1,0:T(8,128)}, u32[]{:S(2)}, u32[]{:S(2)}) collective-permute-start(f32[16,3072]{1,0:T(8,128)S(1)} %fusion), channel_id=1, source_target_pairs={{0,18},{1,19},{2,20},{3,21},{4,22},{5,23},{6,24},{7,25},{8,26},{9,... | collective-permute-start | bytes 589832
  655.6 31.4 %collective-permute-start.16 = (f32[16,3072]{1,0:T(8,128)S(1)}, f32[16,3072]{1,0:T(8,128)}, u32[]{:S(2)}, u32[]{:S(2)}) collective-permute-start(f32[16,3072]{1,0:T(8,128)S(1)} %fusion), channel_id=1, source_target_pairs={{0,17},{1,18},{2,19},{3,20},{4,21},{5,22},{6,23},{7,24},{8,25},{9,... | collective-permute-start | bytes 589832
  657.6 44.1 %collective-permute-start.15 = (f32[16,3072]{1,0:T(8,128)S(1)}, f32[16,3072]{1,0:T(8,128)}, u32[]{:S(2)}, u32[]{:S(2)}) collective-permute-start(f32[16,3072]{1,0:T(8,128)S(1)} %fusion), channel_id=1, source_target_pairs={{0,16},{1,17},{2,18},{3,19},{4,20},{5,21},{6,22},{7,23},{8,24},{9,... | collective-permute-start | bytes 589832
  661.2 67.8 %collective-permute-start.14 = (f32[16,3072]{1,0:T(8,128)S(1)}, f32[16,3072]{1,0:T(8,128)S(1)}, u32[]{:S(2)}, u32[]{:S(2)}) collective-permute-start(f32[16,3072]{1,0:T(8,128)S(1)} %fusion), channel_id=1, source_target_pairs={{0,15},{1,16},{2,17},{3,18},{4,19},{5,20},{6,21},{7,22},{8,23},{9,... | collective-permute-start | bytes 589832
  664.5 65.8 %collective-permute-start.13 = (f32[16,3072]{1,0:T(8,128)S(1)}, f32[16,3072]{1,0:T(8,128)S(1)}, u32[]{:S(2)}, u32[]{:S(2)}) collective-permute-start(f32[16,3072]{1,0:T(8,128)S(1)} %fusion), channel_id=1, source_target_pairs={{0,14},{1,15},{2,16},{3,17},{4,18},{5,19},{6,20},{7,21},{8,22},{9,... | collective-permute-start | bytes 589832
  676.7 58.9 %collective-permute-start.12 = (f32[16,3072]{1,0:T(8,128)S(1)}, f32[16,3072]{1,0:T(8,128)S(1)}, u32[]{:S(2)}, u32[]{:S(2)}) collective-permute-start(f32[16,3072]{1,0:T(8,128)S(1)} %fusion), channel_id=1, source_target_pairs={{0,13},{1,14},{2,15},{3,16},{4,17},{5,18},{6,19},{7,20},{8,21},{9,... | collective-permute-start | bytes 589832
  687.0 50.5 %collective-permute-start.11 = (f32[16,3072]{1,0:T(8,128)S(1)}, f32[16,3072]{1,0:T(8,128)S(1)}, u32[]{:S(2)}, u32[]{:S(2)}) collective-permute-start(f32[16,3072]{1,0:T(8,128)S(1)} %fusion), channel_id=1, source_target_pairs={{0,12},{1,13},{2,14},{3,15},{4,16},{5,17},{6,18},{7,19},{8,20},{9,... | collective-permute-start | bytes 589832
  701.7 38.4 %collective-permute-start.10 = (f32[16,3072]{1,0:T(8,128)S(1)}, f32[16,3072]{1,0:T(8,128)S(1)}, u32[]{:S(2)}, u32[]{:S(2)}) collective-permute-start(f32[16,3072]{1,0:T(8,128)S(1)} %fusion), channel_id=1, source_target_pairs={{0,11},{1,12},{2,13},{3,14},{4,15},{5,16},{6,17},{7,18},{8,19},{9,... | collective-permute-start | bytes 589832
  729.0 23.7 %collective-permute-start.9 = (f32[16,3072]{1,0:T(8,128)S(1)}, f32[16,3072]{1,0:T(8,128)S(1)}, u32[]{:S(2)}, u32[]{:S(2)}) collective-permute-start(f32[16,3072]{1,0:T(8,128)S(1)} %fusion), channel_id=1, source_target_pairs={{0,10},{1,11},{2,12},{3,13},{4,14},{5,15},{6,16},{7,17},{8,18},{9,... | collective-permute-start | bytes 589832
  730.3 29.1 %collective-permute-start.8 = (f32[16,3072]{1,0:T(8,128)S(1)}, f32[16,3072]{1,0:T(8,128)S(1)}, u32[]{:S(2)}, u32[]{:S(2)}) collective-permute-start(f32[16,3072]{1,0:T(8,128)S(1)} %fusion), channel_id=1, source_target_pairs={{0,9},{1,10},{2,11},{3,12},{4,13},{5,14},{6,15},{7,16},{8,17},{9,1... | collective-permute-start | bytes 589832
  735.5 25.8 %collective-permute-start.7 = (f32[16,3072]{1,0:T(8,128)S(1)}, f32[16,3072]{1,0:T(8,128)S(1)}, u32[]{:S(2)}, u32[]{:S(2)}) collective-permute-start(f32[16,3072]{1,0:T(8,128)S(1)} %fusion), channel_id=1, source_target_pairs={{0,8},{1,9},{2,10},{3,11},{4,12},{5,13},{6,14},{7,15},{8,16},{9,17... | collective-permute-start | bytes 589832
  737.5 28.4 %collective-permute-start.6 = (f32[16,3072]{1,0:T(8,128)S(1)}, f32[16,3072]{1,0:T(8,128)S(1)}, u32[]{:S(2)}, u32[]{:S(2)}) collective-permute-start(f32[16,3072]{1,0:T(8,128)S(1)} %fusion), channel_id=1, source_target_pairs={{0,7},{1,8},{2,9},{3,10},{4,11},{5,12},{6,13},{7,14},{8,15},{9,16}... | collective-permute-start | bytes 589832
  740.8 27.1 %collective-permute-start.5 = (f32[16,3072]{1,0:T(8,128)S(1)}, f32[16,3072]{1,0:T(8,128)S(1)}, u32[]{:S(2)}, u32[]{:S(2)}) collective-permute-start(f32[16,3072]{1,0:T(8,128)S(1)} %fusion), channel_id=1, source_target_pairs={{0,6},{1,7},{2,8},{3,9},{4,10},{5,11},{6,12},{7,13},{8,14},{9,15},... | collective-permute-start | bytes 589832
  752.7 25.3 %collective-permute-start.4 = (f32[16,3072]{1,0:T(8,128)S(1)}, f32[16,3072]{1,0:T(8,128)}, u32[]{:S(2)}, u32[]{:S(2)}) collective-permute-start(f32[16,3072]{1,0:T(8,128)S(1)} %fusion), channel_id=1, source_target_pairs={{0,5},{1,6},{2,7},{3,8},{4,9},{5,10},{6,11},{7,12},{8,13},{9,14},{... | collective-permute-start | bytes 589832
  759.4 18.6 %collective-permute-start.3 = (f32[16,3072]{1,0:T(8,128)S(1)}, f32[16,3072]{1,0:T(8,128)}, u32[]{:S(2)}, u32[]{:S(2)}) collective-permute-start(f32[16,3072]{1,0:T(8,128)S(1)} %fusion), channel_id=1, source_target_pairs={{0,4},{1,5},{2,6},{3,7},{4,8},{5,9},{6,10},{7,11},{8,12},{9,13},{1... | collective-permute-start | bytes 589832
  761.4 16.7 %collective-permute-start.2 = (f32[16,3072]{1,0:T(8,128)S(1)}, f32[16,3072]{1,0:T(8,128)}, u32[]{:S(2)}, u32[]{:S(2)}) collective-permute-start(f32[16,3072]{1,0:T(8,128)S(1)} %fusion), channel_id=1, source_target_pairs={{0,3},{1,4},{2,5},{3,6},{4,7},{5,8},{6,9},{7,10},{8,11},{9,12},{10... | collective-permute-start | bytes 589832
  765.9 12.1 %collective-permute-start.1 = (f32[16,3072]{1,0:T(8,128)S(1)}, f32[16,3072]{1,0:T(8,128)}, u32[]{:S(2)}, u32[]{:S(2)}) collective-permute-start(f32[16,3072]{1,0:T(8,128)S(1)} %fusion), channel_id=1, source_target_pairs={{0,2},{1,3},{2,4},{3,5},{4,6},{5,7},{6,8},{7,9},{8,10},{9,11},{10,... | collective-permute-start | bytes 589832
  768.6 9.4 collective-permute-start
  777.9 86.6 %copy-start.47 = (f32[16,48]{1,0:T(8,128)S(1)}, f32[16,48]{1,0:T(8,128)}, u32[]{:S(2)}) copy-start(f32[16,48]{1,0:T(8,128)} %copy-done.46) | copy-start | bytes 9220
  778.0 174.8 %all-gather.3.cloned.1.call-start = ((), (), s32[]{:S(2)}) async-start(), calls=%async_computation.2 | async-start | bytes 3342336 | tf_op jit(solution)/shard_map/all_gather | solution.py:113
  (51 other events, 1410.6 us)
Sparse Core Ops, SparseCore 0:
  778.1 145.1 all-reduce.6
Sparse Core Ops, SparseCore 1:
  864.6 45.1 all-gather.2
